TPU v7x, 32 devices: a whole 2x2x4 slice. The times are simulated.
32 devices in a mesh: batch: 16 (over z, x, core), tensor: 2 (over y).
Axes of the slice: x: 2, y: 2, z: 4, core: 2. Of those that a mesh axis runs over, the one named last changes fastest.
Arguments:
- qkv: bfloat16 [16, 1536, 3, 3072], P('batch', None, None, 'tensor'), may hold values from -18 to 18, as said below
- text_len: int32 [16], replicated, may hold values from 1 to 512, as said below
- step_idx: int32 [16], P('batch'), may hold values from 0 to 27, as said below
- latent: float32 [16, 1024, 64], P('batch', 'tensor'), may hold values from -8 to 8, as said below
- w_out: bfloat16 [3072, 64], replicated, may hold values from -0.109375 to 0.109375
Outputs:
- attn_text: bfloat16 [16, 512, 3072], P('batch', 'tensor')
- velocity: float32 [16, 1024, 64], P('batch', 'tensor')
- new_latent: float32 [16, 1024, 64], P('batch', 'tensor')
Inputs may be any that keep to these rules, and one draw needn't show every extreme that they name: `qkv`: floats of queries, keys and values. `text_len`: copy 2i is a prompt's conditional copy and 2i+1 its unconditional copy. Every conditional copy has 128 or more text tokens and some has 512; every unconditional copy has 64 or fewer and some has exactly 64. `step_idx`: both copies of a prompt carry the same step. Both copies of a prompt carry the same latent.
All inputs are finite; a program needn't handle non-finite values.
Results may differ from a plain program's by a relative error of at most 0.0047.
Values may be sent and summed in bfloat16 or wider, within the bound.
A program may use at most 192 MiB of HBM per device.

v0:
```python
import jax
import jax.numpy as jnp
from jax import lax
from jax.sharding import PartitionSpec as P

HD = 128
TXT = 512
IMG = 1024
NSTEPS = 28


guidance_scale = 3.5
plan_shift = 3.0
norm_eps = 1e-06


def shortened(shard):
    return jax.tree.map(lambda a: a.astype(jnp.bfloat16) if a.dtype == jnp.float32 else a, shard)


def from_partner(value, axis, apart):
    mask = 2**apart
    pairs = [(source, source ^ mask) for source in range(lax.axis_size(axis))]
    return lax.ppermute(value, axis, pairs)


def sigma_at(step_value):
    remain = 1.0 - step_value / NSTEPS
    return plan_shift * remain / (1.0 + (plan_shift - 1.0) * remain)


def attend_block(queries, keys, values, text_length):
    score_scale = HD ** (-0.5)
    row_count = queries.shape[0]
    head_count = queries.shape[1]
    image_keys = keys[TXT:]
    image_values = values[TXT:]
    image_scores = (
        jnp.einsum("rhd,khd->hrk", queries, image_keys, preferred_element_type=jnp.float32)
        * score_scale
    )
    block_width = min(128, TXT)
    block_count = TXT // block_width
    text_scores = []
    for block_index in range(block_count):
        block_start = block_index * block_width
        key_part = keys[block_start : block_start + block_width]

        def compute_block(key_part=key_part, block_start=block_start):
            score_part = (
                jnp.einsum("rhd,khd->hrk", queries, key_part, preferred_element_type=jnp.float32)
                * score_scale
            )
            column = block_start + lax.broadcasted_iota(jnp.int32, score_part.shape, 2)
            return jnp.where(column < text_length, score_part, -jnp.inf)

        def empty_block():
            return jnp.full((head_count, row_count, block_width), -jnp.inf, jnp.float32)

        text_scores.append(lax.cond(block_start < text_length, compute_block, empty_block))
    row_max = jnp.max(image_scores, axis=2, keepdims=True)
    for score_part in text_scores:
        row_max = jnp.maximum(row_max, jnp.max(score_part, axis=2, keepdims=True))
    weights = jnp.exp(image_scores - row_max)
    denominator = jnp.sum(weights, axis=2, keepdims=True)
    summed = jnp.einsum(
        "hrk,khd->hrd",
        weights.astype(jnp.bfloat16),
        image_values,
        preferred_element_type=jnp.float32,
    )
    for block_index in range(block_count):
        block_start = block_index * block_width
        value_part = values[block_start : block_start + block_width]
        text_weights = jnp.exp(text_scores[block_index] - row_max)
        denominator = denominator + jnp.sum(text_weights, axis=2, keepdims=True)

        def add_values(text_weights=text_weights, value_part=value_part):
            return jnp.einsum(
                "hrk,khd->hrd",
                text_weights.astype(jnp.bfloat16),
                value_part,
                preferred_element_type=jnp.float32,
            )

        def no_values():
            return jnp.zeros((head_count, row_count, HD), jnp.float32)

        summed = summed + lax.cond(block_start < text_length, add_values, no_values)
    result = (summed / denominator).astype(jnp.bfloat16)
    return jnp.transpose(result, (1, 0, 2))


def attend_rows(queries, keys, values, text_length):
    row_count = queries.shape[0]
    block_rows = min(512, row_count)
    grouped = queries.reshape(
        row_count // block_rows, block_rows, queries.shape[1], queries.shape[2]
    )

    def one_block(query_block):
        return attend_block(query_block, keys, values, text_length)

    return lax.map(one_block, grouped).reshape(queries.shape)


def per_device(qkv, text_len, step_idx, latent, w_out):
    local = qkv[0]
    seq_len = local.shape[0]
    head_count = local.shape[2] // HD
    local_width = head_count * HD
    queries = local[:, 0].reshape(seq_len, head_count, HD)
    keys = local[:, 1].reshape(seq_len, head_count, HD)
    values = local[:, 2].reshape(seq_len, head_count, HD)
    position = lax.axis_index("batch")
    parity = position % 2
    own_length = text_len[position]
    text_out = attend_rows(queries[:TXT], keys, values, own_length)
    text_rows = lax.broadcasted_iota(jnp.int32, (TXT, 1, 1), 0)
    text_out = jnp.where(text_rows < own_length, text_out, jnp.zeros((), jnp.bfloat16))
    image_out = attend_rows(queries[TXT:], keys, values, own_length)
    text_flat = text_out.reshape(1, TXT, local_width)
    colsum = jnp.sum(w_out.astype(jnp.float32), axis=0)[None, :]
    image_flat = image_out.reshape(1, IMG, local_width)
    text_tokens, image_tokens = (
        lax.all_to_all(
            shortened(text_flat), "tensor", split_axis=1, concat_axis=2, tiled=True
        ).astype(text_flat.dtype),
        lax.all_to_all(
            shortened(image_flat), "tensor", split_axis=1, concat_axis=2, tiled=True
        ).astype(image_flat.dtype),
    )
    token_rows = image_tokens[0]
    hidden = token_rows.astype(jnp.float32)
    row_mean = jnp.mean(hidden, axis=1, keepdims=True)
    row_meansq = jnp.mean(hidden * hidden, axis=1, keepdims=True)
    product = jnp.dot(token_rows, w_out, preferred_element_type=jnp.float32)
    raw_velocity = (product - row_mean * colsum) * lax.rsqrt(
        row_meansq - row_mean * row_mean + norm_eps
    )
    partner_velocity = from_partner(shortened(raw_velocity), "batch", 0).astype(raw_velocity.dtype)
    is_cond = parity == 0
    cond_velocity = jnp.where(is_cond, raw_velocity, partner_velocity)
    uncond_velocity = jnp.where(is_cond, partner_velocity, raw_velocity)
    guided = uncond_velocity + guidance_scale * (cond_velocity - uncond_velocity)
    step_value = step_idx[0].astype(jnp.float32)
    step_delta = sigma_at(step_value + 1.0) - sigma_at(step_value)
    updated = latent[0] + step_delta * guided
    return (text_tokens, guided[None], updated[None])


def solution(mesh):
    placed = (P("batch", None, None, "tensor"), P(), P("batch"), P("batch", "tensor", None), P())
    return jax.shard_map(
        per_device,
        mesh=mesh,
        in_specs=placed,
        out_specs=(
            P("batch", "tensor", None),
            P("batch", "tensor", None),
            P("batch", "tensor", None),
        ),
        check_vma=False,
    )
```

profile of v0, /device:TPU:29, one launch (start us, length us, event | category | flops | bytes accessed | tf_op | source)
XLA Modules:
  0.0 460.0 jit_solution(4597364450118867338)
XLA Ops:
  0.6 18.6 %copy.136 = bf16[1,1536,3,1536]{1,3,2,0:T(8,128)(2,1)} copy(bf16[1,1536,3,1536]{3,1,2,0:T(8,128)(2,1)} %param.39) | data formatting | bytes 28311552 | tf_op args[0]
  19.3 6.1 %fusion.79 = (bf16[1024,1,1536]{0,2,1:T(8,128)(2,1)S(1)}, bf16[1024,1,1536]{0,2,1:T(8,128)(2,1)}, bf16[1024,1,1536]{0,2,1:T(8,128)(2,1)}) fusion(bf16[1536,3,1536]{0,2,1:T(8,128)(2,1)} %bitcast.120), kind=kLoop, calls=%fused_computation.118 | loop fusion | bytes 18874368 | tf_op jit(solution)/shard_map/slice | solution.py:121
  25.3 8.0 %fusion.78 = (bf16[1536,1,1536]{0,2,1:T(8,128)(2,1)}, bf16[1536,1,1536]{0,2,1:T(8,128)(2,1)}) fusion(bf16[1536,3,1536]{0,2,1:T(8,128)(2,1)} %bitcast.121), kind=kLoop, calls=%fused_computation.117 | loop fusion | bytes 18874368 | tf_op jit(solution)/shard_map/slice | solution.py:114
  36.5 4.0 reshape.181
  40.5 8.7 %copy.153 = bf16[2,512,12,128]{3,1,2,0:T(8,128)(2,1)} copy(bf16[2,512,12,128]{1,0,3,2:T(2,128)(2,1)} %reshape.181) | data formatting | bytes 6291456 | tf_op jit(solution)/shard_map/while | solution.py:104
  49.2 6.7 %copy.154 = bf16[1536,12,128]{2,0,1:T(8,128)(2,1)} copy(bf16[1536,12,128]{0,2,1:T(8,128)(2,1)} %bitcast.142) | data formatting | bytes 9437184 | tf_op jit(solution)/shard_map/while | solution.py:104
  55.8 6.6 %copy.155 = bf16[1536,12,128]{2,0,1:T(8,128)(2,1)} copy(bf16[1536,12,128]{0,2,1:T(8,128)(2,1)} %bitcast.141) | data formatting | bytes 9437184 | tf_op jit(solution)/shard_map/while | solution.py:104
  62.4 147.2 %while.3 = (s32[]{:T(128)}, bf16[2,512,12,128]{3,1,2,0:T(8,128)(2,1)}, bf16[2,512,12,128]{3,1,2,0:T(8,128)(2,1)}, bf16[1536,12,128]{2,0,1:T(8,128)(2,1)}, pred[]...) while((s32[]{:T(128)}, ...), condition=%wide.region_53.54_spmd, body=%wide.region_26.53_spmd.sunk | while | flops 4905751552 | bytes 186238320 | solution.py:104
  64.1 7.6 %conditional.32 = (f32[12,512,1]{1,0,2:T(8,128)S(1)}, f32[12,512,128]{2,1,0:T(8,128)}) conditional(s32[]{:T(128)} %convert_element_type.165, () %tuple.270, (s32[]{:T(128)}, bf16[1536,12,128]{2,0,1:T(8,128)(2,1)}, bf16[512,12,128]{2,0,1:T(8,128)(2,1)S(1)}) %tuple.271), branch_computations={%region_28.28_spmd, %region_29.30_spmd} | conditional | flops 203679872 | bytes 11428116 | solution.py:60
  64.8 3.3 fusion.74
  68.1 3.6 copy.176
  77.6 12.0 %multiply_reduce_fusion.3 = (f32[12,512]{1,0:T(8,128)S(1)}, f32[12,512,1024]{2,1,0:T(8,128)}) fusion(bf16[512,12,128]{2,0,1:T(8,128)(2,1)S(1)} %dynamic-slice_bitcast_fusion.2, bf16[1536,12,128]{2,0,1:T(8,128)(2,1)} %get-tuple-element.678), kind=kOutput, calls=%fused_computation.41.clone.1 | convolution fusion | flops 1623189504 | bytes 29908992 | tf_op jit(solution)/shard_map/while/body/eval_jaxpr/rhd,khd->hrk/dot_general | solution.py:39
  89.6 9.4 %fusion.122 = (f32[12,512]{1,0:T(8,128)S(1)}, bf16[12,512,128]{2,1,0:T(8,128)(2,1)S(1)}, f32[12,512]{1,0:T(8,128)S(1)}, bf16[12,512,128]{2,1,0:T(8,128)(2,1)S(1)...) fusion(f32[12,512,128]{2,1,0:T(8,128)} %get-tuple-element.595, ...), kind=kLoop, calls=%fused_computation.101.clone.1 | loop fusion | flops 9412608 | bytes 18997248 | tf_op jit(solution)/shard_map/while/body/eval_jaxpr/reduce_sum | solution.py:76
  99.0 11.0 %fusion.123 = f32[12,512]{1,0:T(8,128)S(1)} fusion(f32[12,512,1024]{2,1,0:T(8,128)} %get-tuple-element.607, f32[12,512]{1,0:T(8,128)S(1)} %fusion.121), kind=kLoop, calls=%fused_computation.42.clone.1 | loop fusion | flops 18868224 | bytes 25214976 | tf_op jit(solution)/shard_map/while/body/eval_jaxpr/reduce_sum | solution.py:65
  115.9 3.3 conditional.39
  115.9 3.3 fusion.12
  119.2 16.7 %bitcast_dynamic-update-slice_fusion.2 = bf16[2,512,12,128]{3,1,2,0:T(8,128)(2,1)} fusion(bf16[2,512,12,128]{3,1,2,0:T(8,128)(2,1)} %get-tuple-element.665, s32[]{:T(128)S(6)} %copy.253, f32[12,512]{1,0:T(8,128)S(1)} %add_add_fusion.3, f32[12,512,128]{2,1,0:T(8,128)} %get-tuple-element.686, f32[12,512,128]{2,1,0:T(8,128)} %get-tuple-element.687, ...), kind=kOutput, calls=%fused_computation.55.clone.1 | convolution fusion | flops 1634205696 | bytes 42516484 | tf_op jit(solution)/shard_map/while/body/eval_jaxpr/hrk,khd->hrd/dot_general | solution.py:66
  137.4 7.6 %conditional.32 = (f32[12,512,1]{1,0,2:T(8,128)S(1)}, f32[12,512,128]{2,1,0:T(8,128)}) conditional(s32[]{:T(128)} %convert_element_type.165, () %tuple.270, (s32[]{:T(128)}, bf16[1536,12,128]{2,0,1:T(8,128)(2,1)}, bf16[512,12,128]{2,0,1:T(8,128)(2,1)S(1)}) %tuple.271), branch_computations={%region_28.28_spmd, %region_29.30_spmd} | conditional | flops 203679872 | bytes 11428116 | solution.py:60
  138.1 3.2 fusion.74
  141.4 3.6 copy.176
  150.9 12.0 %multiply_reduce_fusion.3 = (f32[12,512]{1,0:T(8,128)S(1)}, f32[12,512,1024]{2,1,0:T(8,128)}) fusion(bf16[512,12,128]{2,0,1:T(8,128)(2,1)S(1)} %dynamic-slice_bitcast_fusion.2, bf16[1536,12,128]{2,0,1:T(8,128)(2,1)} %get-tuple-element.678), kind=kOutput, calls=%fused_computation.41.clone.1 | convolution fusion | flops 1623189504 | bytes 29908992 | tf_op jit(solution)/shard_map/while/body/eval_jaxpr/rhd,khd->hrk/dot_general | solution.py:39
  162.9 9.4 %fusion.122 = (f32[12,512]{1,0:T(8,128)S(1)}, bf16[12,512,128]{2,1,0:T(8,128)(2,1)S(1)}, f32[12,512]{1,0:T(8,128)S(1)}, bf16[12,512,128]{2,1,0:T(8,128)(2,1)S(1)...) fusion(f32[12,512,128]{2,1,0:T(8,128)} %get-tuple-element.595, ...), kind=kLoop, calls=%fused_computation.101.clone.1 | loop fusion | flops 9412608 | bytes 18997248 | tf_op jit(solution)/shard_map/while/body/eval_jaxpr/reduce_sum | solution.py:76
  172.3 11.0 %fusion.123 = f32[12,512]{1,0:T(8,128)S(1)} fusion(f32[12,512,1024]{2,1,0:T(8,128)} %get-tuple-element.607, f32[12,512]{1,0:T(8,128)S(1)} %fusion.121), kind=kLoop, calls=%fused_computation.42.clone.1 | loop fusion | flops 18868224 | bytes 25214976 | tf_op jit(solution)/shard_map/while/body/eval_jaxpr/reduce_sum | solution.py:65
  189.2 3.3 conditional.39
  189.2 3.3 fusion.12
  192.5 16.7 %bitcast_dynamic-update-slice_fusion.2 = bf16[2,512,12,128]{3,1,2,0:T(8,128)(2,1)} fusion(bf16[2,512,12,128]{3,1,2,0:T(8,128)(2,1)} %get-tuple-element.665, s32[]{:T(128)S(6)} %copy.253, f32[12,512]{1,0:T(8,128)S(1)} %add_add_fusion.3, f32[12,512,128]{2,1,0:T(8,128)} %get-tuple-element.686, f32[12,512,128]{2,1,0:T(8,128)} %get-tuple-element.687, ...), kind=kOutput, calls=%fused_computation.55.clone.1 | convolution fusion | flops 1634205696 | bytes 42516484 | tf_op jit(solution)/shard_map/while/body/eval_jaxpr/hrk,khd->hrd/dot_general | solution.py:66
  209.6 6.1 %copy.174 = bf16[2,512,12,128]{3,2,1,0:T(8,128)(2,1)} copy(bf16[2,512,12,128]{3,1,2,0:T(8,128)(2,1)} %get-tuple-element.315) | data formatting | bytes 6291456 | tf_op jit(solution)/shard_map/reshape;reshape | solution.py:124
  215.7 19.0 %reshape.193 = bf16[1,1024,1536]{2,0,1:T(2,128)(2,1)} reshape(bf16[2,512,12,128]{3,2,1,0:T(8,128)(2,1)} %copy.174) | data formatting | bytes 6291456 | tf_op jit(solution)/shard_map/reshape;reshape | solution.py:124
  235.3 20.3 %reduce.3 = bf16[1024,1536]{1,0:T(8,128)(2,1)S(1)} reduce(bf16[1024,1,1536]{2,1,0:T(2,128)(2,1)} %bitcast.139, bf16[]{:T(256)} %broadcast.220), dimensions={1}, to_apply=%bitcast.77.reduce_sub_computation | reduce | bytes 6291458
  255.6 3.4 reshape.196
  259.0 5.4 %all-to-all-start.1 = ((bf16[2,2,393216]{2,1,0:T(2,128)(2,1)}), bf16[2,2,393216]{2,1,0:T(2,128)(2,1)}, u32[]{:S(2)}, u32[]{:S(2)}) async-start(bf16[2,2,393216]{2,1,0:T(2,128)(2,1)} %reshape.196), calls=%async_computation.1 | async-start | bytes 6291456 | tf_op jit(solution)/shard_map/all_to_all | solution.py:129
  265.9 12.1 %multiply_reduce_fusion.1 = (f32[12,512]{1,0:T(8,128)S(1)}, f32[12,512,1024]{2,1,0:T(8,128)}) fusion(bf16[512,12,128]{0,2,1:T(8,128)(2,1)S(1)} %bitcast.131, bf16[1024,12,128]{0,2,1:T(8,128)(2,1)} %bitcast.138), kind=kOutput, calls=%fused_computation.65 | convolution fusion | flops 1623189504 | bytes 29908992 | tf_op jit(solution)/shard_map/while/body/eval_jaxpr/rhd,khd->hrk/dot_general | solution.py:39
  278.0 7.7 %conditional.16 = (f32[12,512,1]{1,0,2:T(8,128)S(1)}, f32[12,512,128]{2,1,0:T(8,128)}) conditional(s32[]{:T(128)} %convert_element_type.98, () %tuple.146, (s32[]{:T(128)}, bf16[1536,3,1536]{0,2,1:T(8,128)(2,1)}, bf16[512,12,128]{0,2,1:T(8,128)(2,1)S(1)}) %tuple.326), branch_computations={%region_1.2_spmd, %region_2.4_spmd} | conditional | flops 203679872 | bytes 12214548 | solution.py:60
  279.7 2.4 fusion.70
  282.2 3.6 copy.184
  291.9 9.0 %fusion.66 = (f32[12,512]{1,0:T(8,128)S(1)}, bf16[12,512,128]{2,1,0:T(8,128)(2,1)S(1)}, f32[12,512]{1,0:T(8,128)S(1)}, bf16[12,512,128]{2,1,0:T(8,128)(2,1)S(1)}...) fusion(f32[12,512,128]{2,1,0:T(8,128)} %get-tuple-element.411, ...), kind=kLoop, calls=%fused_computation.105 | loop fusion | flops 9412608 | bytes 18997248 | tf_op jit(solution)/shard_map/while/body/eval_jaxpr/reduce_sum | solution.py:76
  300.9 11.0 %fusion.42 = f32[12,512]{1,0:T(8,128)S(1)} fusion(f32[12,512,1024]{2,1,0:T(8,128)} %get-tuple-element.497, f32[12,512]{1,0:T(8,128)S(1)} %fusion.60), kind=kLoop, calls=%fused_computation.66 | loop fusion | flops 18868224 | bytes 25214976 | tf_op jit(solution)/shard_map/while/body/eval_jaxpr/reduce_sum | solution.py:65
  318.1 3.3 conditional.20
  321.4 16.6 %divide_convert_fusion.1 = bf16[12,512,128]{1,2,0:T(8,128)(2,1)} fusion(f32[12,512,128]{1,2,0:T(8,128)} %copy-done.1, f32[12,512,128]{1,2,0:T(8,128)} %copy-done.2, f32[12,512,128]{1,2,0:T(8,128)} %copy-done.3, f32[12,512,128]{1,2,0:T(8,128)} %get-tuple-element.415, bf16[1024,12,128]{0,2,1:T(8,128)(2,1)} %bitcast.151, ...), kind=kOutput, calls=%fused_computation.75 | convolution fusion | flops 1634205696 | bytes 42516480 | tf_op jit(solution)/shard_map/while/body/eval_jaxpr/hrk,khd->hrd/dot_general | solution.py:66
  338.1 7.0 %copy.151 = bf16[1,512,1536]{2,0,1:T(2,128)(2,1)S(1)} copy(bf16[1,512,1536]{1,2,0:T(8,128)(2,1)} %bitcast.156) | data formatting | bytes 3145728 | tf_op jit(solution)/shard_map/reshape | solution.py:104
  345.7 5.8 %fusion.81 = bf16[512,1,1536]{2,1,0:T(2,128)(2,1)} fusion(bf16[1,512,1536]{2,0,1:T(2,128)(2,1)S(1)} %copy.151, pred[512]{0:T(512)(128)(4,1)S(1)} %iota_compare_fusion.2), kind=kLoop, calls=%fused_computation.120 | loop fusion | flops 786432 | bytes 3146240
  351.5 11.3 %reduce.2 = bf16[512,1536]{1,0:T(8,128)(2,1)S(1)} reduce(bf16[512,1,1536]{2,1,0:T(2,128)(2,1)} %fusion.81, bf16[]{:T(256)} %broadcast.220), dimensions={1}, to_apply=%fusion.81.reduce_sub_computation | reduce | bytes 3145730
  365.1 4.7 %all-to-all-start = ((bf16[2,2,196608]{2,1,0:T(2,128)(2,1)}), bf16[2,2,196608]{2,1,0:T(2,128)(2,1)}, u32[]{:S(2)}, u32[]{:S(2)}) async-start(bf16[2,2,196608]{2,1,0:T(2,128)(2,1)} %reshape.194), calls=%async_computation | async-start | bytes 3145728 | tf_op jit(solution)/shard_map/all_to_all | solution.py:126
  369.7 6.0 %reshape.197 = bf16[1024,1,1536]{2,1,0:T(2,128)(2,1)} reshape(bf16[2,2,393216]{2,1,0:T(2,128)(2,1)} %all-to-all-done.1) | data formatting | bytes 6291456
  375.7 3.6 copy.201
  379.3 2.8 copy.158
  385.4 65.4 %collective-permute-start = (bf16[512,64]{0,1:T(8,128)(2,1)}, bf16[512,64]{0,1:T(8,128)(2,1)S(1)}, u32[]{:S(2)}, u32[]{:S(2)}) collective-permute-start(bf16[512,64]{0,1:T(8,128)(2,1)} %get-tuple-element.498), channel_id=1, source_target_pairs={{0,2},{2,0},{4,6},{6,4},{8,10},{10,8},{12,14},{14,12},{16,18},{18,... | collective-permute-start | bytes 196616 | tf_op jit(solution)/shard_map/ppermute | solution.py:24
  451.5 2.5 reshape.195
  (92 shorter events, 90.4 us)
Async XLA Ops:
  25.3 8.0 %copy-start.7 = (s32[16]{0:T(128)S(1)}, s32[16]{0:T(128)}, u32[]{:S(2)}) copy-start(s32[16]{0:T(128)} %param.40) | copy-start | bytes 196
  259.0 106.1 %all-to-all-start.1 = ((bf16[2,2,393216]{2,1,0:T(2,128)(2,1)}), bf16[2,2,393216]{2,1,0:T(2,128)(2,1)}, u32[]{:S(2)}, u32[]{:S(2)}) async-start(bf16[2,2,393216]{2,1,0:T(2,128)(2,1)} %reshape.196), calls=%async_computation.1 | async-start | bytes 6291456 | tf_op jit(solution)/shard_map/all_to_all | solution.py:129
  312.4 1.7 copy-start.1
  314.4 1.7 copy-start.2
  316.5 1.6 copy-start.3
  351.5 13.4 %copy-start.4 = (bf16[3072,64]{0,1:T(8,128)(2,1)S(1)}, bf16[3072,64]{0,1:T(8,128)(2,1)}, u32[]{:S(2)}) copy-start(bf16[3072,64]{0,1:T(8,128)(2,1)} %param.43) | copy-start | bytes 1179652
  365.1 86.4 %all-to-all-start = ((bf16[2,2,196608]{2,1,0:T(2,128)(2,1)}), bf16[2,2,196608]{2,1,0:T(2,128)(2,1)}, u32[]{:S(2)}, u32[]{:S(2)}) async-start(bf16[2,2,196608]{2,1,0:T(2,128)(2,1)} %reshape.194), calls=%async_computation | async-start | bytes 3145728 | tf_op jit(solution)/shard_map/all_to_all | solution.py:126
  382.2 1.9 copy-start
  385.4 73.6 %collective-permute-start = (bf16[512,64]{0,1:T(8,128)(2,1)}, bf16[512,64]{0,1:T(8,128)(2,1)S(1)}, u32[]{:S(2)}, u32[]{:S(2)}) collective-permute-start(bf16[512,64]{0,1:T(8,128)(2,1)} %get-tuple-element.498), channel_id=1, source_target_pairs={{0,2},{2,0},{4,6},{6,4},{8,10},{10,8},{12,14},{14,12},{16,18},{18,... | collective-permute-start | bytes 196616 | tf_op jit(solution)/shard_map/ppermute | solution.py:24
  455.5 3.5 copy-start.5
  455.5 3.5 copy-start.6
where the time goes:
time: 466 us; the launch traced here: 460 us
  local copies, waits for them, and re-layouts  171 us (37%)
  matrix products  105 us (23%)
  other arithmetic  103 us (22%)
  starting transfers between devices  75.4 us (16%)
    ppermute x1, starting transfers between devices, from_partner(): return lax.ppermute(value, axis, pairs)  65.4 us
    dot_general x3, matrix products, attend_block(): jnp.einsum('hrk,khd->hrd', weights.astype(jnp.bfloat16), image_values, pr...  50 us
    unnamed x25, local copies, waits for them, and re-layouts  45.8 us
    unnamed x3, other arithmetic  37.4 us
    dot_general x3, matrix products, attend_block(): jnp.einsum('rhd,khd->hrk', queries, image_keys, preferred_element_type=jn...  36 us
    reduce_sum x3, other arithmetic, attend_block(): denominator = jnp.sum(weights, axis=2, keepdims=True)  33 us
    another operation x18, local copies, waits for them, and re-layouts  30.6 us
    reduce_sum x3, other arithmetic, attend_block(): denominator = denominator + jnp.sum(text_weights, axis=2, keepdims=True)  27.8 us
  transfers between devices with their start and end apart: 3, of which 0 were waited for; matrix products, arithmetic and copies ran while one was open for 26% of the time, Pallas kernels for 0%

commit v1 on v0

v1 whole, which is shorter than its diff:
```python
import functools

import jax
import jax.numpy as jnp
from jax import lax
from jax.experimental import pallas as pl
from jax.experimental.pallas import tpu as pltpu
from jax.sharding import PartitionSpec as P

HD = 128
TXT = 512
NSTEPS = 28

guidance_scale = 3.5
plan_shift = 3.0
norm_eps = 1e-06

LOG2_SCALE = 1.4426950408889634 * HD ** (-0.5)
ROWS = 256
CONTRACT_LAST = (((1,), (1,)), ((), ()))


def sigma_at(step_value):
    remain = 1.0 - step_value / NSTEPS
    return plan_shift * remain / (1.0 + (plan_shift - 1.0) * remain)


def prepare_keys(text_length, k_ref, v_ref, kk, vv):
    seq = k_ref.shape[1]
    keys = k_ref[0]
    row = lax.broadcasted_iota(jnp.int32, (TXT, HD), 0)
    valid = row < text_length
    spare = jnp.broadcast_to(keys[TXT : TXT + 1].astype(jnp.float32), (TXT, HD))
    text_keys = jnp.where(valid, keys[:TXT].astype(jnp.float32), spare).astype(jnp.bfloat16)
    kk[:TXT, :HD] = text_keys
    kk[:TXT, HD:] = text_keys
    kk[TXT:, :HD] = keys[TXT:]
    kk[TXT:, HD:] = keys[TXT:]
    text_values = jnp.where(valid, v_ref[0, :TXT].astype(jnp.float32), 0.0)
    vv[:TXT, :HD] = text_values.astype(jnp.bfloat16)
    vv[:TXT, HD:] = jnp.where(valid, 1.0, 0.0).astype(jnp.bfloat16)
    vv[TXT:, :HD] = v_ref[0, TXT:]
    vv[TXT:, HD:] = jnp.ones((seq - TXT, HD), jnp.bfloat16)


def attend(query, kk, vv):
    scaled = query.astype(jnp.float32) * LOG2_SCALE
    high = scaled.astype(jnp.bfloat16)
    low = (scaled - high.astype(jnp.float32)).astype(jnp.bfloat16)
    both = jnp.concatenate([high, low], axis=1)
    scores = lax.dot_general(both, kk[...], CONTRACT_LAST, preferred_element_type=jnp.float32)
    row_max = jnp.max(scores, axis=1, keepdims=True)
    weights = jnp.exp2(scores - row_max).astype(jnp.bfloat16)
    summed = jnp.dot(weights, vv[...], preferred_element_type=jnp.float32)
    return (summed[:, :HD] / summed[:, HD:]).astype(jnp.bfloat16)


def text_kernel(length_ref, q_ref, k_ref, v_ref, out_ref, kk, vv):
    text_length = length_ref[0]
    prepare_keys(text_length, k_ref, v_ref, kk, vv)
    for start in range(0, TXT, ROWS):
        result = attend(q_ref[0, start : start + ROWS], kk, vv)
        row = start + lax.broadcasted_iota(jnp.int32, (ROWS, HD), 0)
        kept = jnp.where(row < text_length, result.astype(jnp.float32), 0.0)
        out_ref[start : start + ROWS, :] = kept.astype(jnp.bfloat16)


def image_kernel(length_ref, q_ref, k_ref, v_ref, w_ref, out_ref, kk, vv):
    image = out_ref.shape[1]

    @pl.when(pl.program_id(0) == 0)
    def _():
        out_ref[...] = jnp.zeros_like(out_ref)

    prepare_keys(length_ref[0], k_ref, v_ref, kk, vv)
    ones = jnp.ones((8, 2 * HD), jnp.bfloat16)
    for start in range(0, image, ROWS):
        result = attend(q_ref[0, TXT + start : TXT + start + ROWS], kk, vv)
        wide = result.astype(jnp.float32)
        square = wide * wide
        high = square.astype(jnp.bfloat16)
        low = (square - high.astype(jnp.float32)).astype(jnp.bfloat16)
        squares = jnp.concatenate([high, low], axis=1)
        span = slice(start, start + ROWS)
        out_ref[:72, span] += lax.dot_general(
            w_ref[...], result, CONTRACT_LAST, preferred_element_type=jnp.float32
        )
        out_ref[72:, span] += lax.dot_general(
            ones, squares, CONTRACT_LAST, preferred_element_type=jnp.float32
        )


def head_specs(seq):
    def part(which):
        return pl.BlockSpec((1, seq, HD), lambda h, length: (which, 0, h))

    return [part(0), part(1), part(2)]


def scratch(seq):
    return [pltpu.VMEM((seq, 2 * HD), jnp.bfloat16), pltpu.VMEM((seq, 2 * HD), jnp.bfloat16)]


def cost(heads, rows, seq):
    return pl.CostEstimate(
        flops=8 * heads * rows * seq * HD,
        bytes_accessed=6 * heads * seq * HD,
        transcendentals=heads * rows * seq,
    )


def attend_text(length, local):
    seq, width = local.shape[1:]
    heads = width // HD
    return pl.pallas_call(
        text_kernel,
        grid_spec=pltpu.PrefetchScalarGridSpec(
            num_scalar_prefetch=1,
            grid=(heads,),
            in_specs=head_specs(seq),
            out_specs=pl.BlockSpec((TXT, HD), lambda h, length: (0, h)),
            scratch_shapes=scratch(seq),
        ),
        out_shape=jax.ShapeDtypeStruct((TXT, width), jnp.bfloat16),
        compiler_params=pltpu.CompilerParams(vmem_limit_bytes=40 * 2**20),
        cost_estimate=cost(heads, TXT, seq),
    )(length, local, local, local)


def attend_image(length, local, weight):
    seq, width = local.shape[1:]
    heads = width // HD
    image = seq - TXT
    return pl.pallas_call(
        image_kernel,
        grid_spec=pltpu.PrefetchScalarGridSpec(
            num_scalar_prefetch=1,
            grid=(heads,),
            in_specs=head_specs(seq) + [pl.BlockSpec((72, HD), lambda h, length: (0, h))],
            out_specs=pl.BlockSpec((80, image), lambda h, length: (0, 0)),
            scratch_shapes=scratch(seq),
        ),
        out_shape=jax.ShapeDtypeStruct((80, image), jnp.float32),
        compiler_params=pltpu.CompilerParams(vmem_limit_bytes=40 * 2**20),
        cost_estimate=cost(heads, image, seq),
    )(length, local, local, local, weight)


def per_device(qkv, text_len, step_idx, latent, w_out):
    local = jnp.transpose(qkv[0], (1, 0, 2))
    width = local.shape[2]
    shares = lax.axis_size("tensor")
    position = lax.axis_index("batch")
    share = lax.axis_index("tensor")
    length = lax.dynamic_slice_in_dim(text_len, position, 1)

    text_out = attend_text(length, local)
    text_rows = TXT // shares
    if shares == 2:
        kept = lax.dynamic_slice_in_dim(text_out, share * text_rows, text_rows)
        sent = lax.dynamic_slice_in_dim(text_out, (1 - share) * text_rows, text_rows)
        came = lax.ppermute(sent, "tensor", [(0, 1), (1, 0)])
        first = share == 0
        text_tokens = jnp.concatenate(
            [jnp.where(first, kept, came), jnp.where(first, came, kept)], axis=1
        )
    else:
        text_tokens = lax.all_to_all(text_out, "tensor", split_axis=0, concat_axis=1, tiled=True)

    weight_t = jnp.transpose(w_out)
    own = lax.dynamic_slice_in_dim(weight_t, share * width, width, axis=1)
    own = jnp.concatenate([own, jnp.ones((8, width), jnp.bfloat16)], axis=0)
    sums = attend_image(length, local, own)
    sums = jnp.concatenate([sums[:65], sums[72:73]], axis=0)
    image_rows = sums.shape[1] // shares
    if shares == 2:
        kept = lax.dynamic_slice_in_dim(sums, share * image_rows, image_rows, axis=1)
        sent = lax.dynamic_slice_in_dim(sums, (1 - share) * image_rows, image_rows, axis=1)
        total = kept + lax.ppermute(sent, "tensor", [(0, 1), (1, 0)])
    else:
        total = lax.psum_scatter(sums, "tensor", scatter_dimension=1, tiled=True)

    depth = w_out.shape[0]
    colsum = jnp.sum(weight_t.astype(jnp.float32), axis=1, keepdims=True)
    row_mean = total[64:65] / depth
    row_meansq = total[65:66] / depth
    raw = (total[:64] - row_mean * colsum) * lax.rsqrt(row_meansq - row_mean * row_mean + norm_eps)
    pairs = [(source, source ^ 1) for source in range(lax.axis_size("batch"))]
    partner = lax.ppermute(raw.astype(jnp.bfloat16), "batch", pairs).astype(jnp.float32)
    is_cond = position % 2 == 0
    cond_velocity = jnp.where(is_cond, raw, partner)
    uncond_velocity = jnp.where(is_cond, partner, raw)
    guided = uncond_velocity + guidance_scale * (cond_velocity - uncond_velocity)
    step_value = step_idx[0].astype(jnp.float32)
    step_delta = sigma_at(step_value + 1.0) - sigma_at(step_value)
    updated = jnp.transpose(latent[0]) + step_delta * guided
    return (text_tokens[None], jnp.transpose(guided)[None], jnp.transpose(updated)[None])


def solution(mesh):
    placed = (P("batch", None, None, "tensor"), P(), P("batch"), P("batch", "tensor", None), P())
    return jax.shard_map(
        per_device,
        mesh=mesh,
        in_specs=placed,
        out_specs=(
            P("batch", "tensor", None),
            P("batch", "tensor", None),
            P("batch", "tensor", None),
        ),
        check_vma=False,
    )
```

time: 466 us -> 110 us (0.24)
  the two profiles are of different devices: /device:TPU:29 before, /device:TPU:0 now
where the time goes in v1:
time: 110 us
  Pallas kernels  81.6 us (74%)
  waiting for transfers between devices  16.3 us (15%)
  other arithmetic  3.98 us (4%)
  starting transfers between devices  3.13 us (3%)
  local copies, waits for them, and re-layouts  3.12 us (3%)
  between operations  1.48 us (1%)
    pallas_call x1, Pallas kernels, attend_image(): pl.pallas_call(image_kernel, grid_spec=pltpu.PrefetchScalarGridSpec(num_s...  59.4 us
    pallas_call x1, Pallas kernels, attend_text(): pl.pallas_call(text_kernel, grid_spec=pltpu.PrefetchScalarGridSpec(num_sc...  22.3 us
    ppermute x1, waiting for transfers between devices, per_device(): came = lax.ppermute(sent, 'tensor', [(0, 1), (1, 0)])  15.8 us
    ppermute x1, starting transfers between devices, per_device(): total = kept + lax.ppermute(sent, 'tensor', [(0, 1), (1, 0)])  2.98 us
  transfers between devices with their start and end apart: 3, of which 2 were waited for; matrix products, arithmetic and copies ran while one was open for 1% of the time, Pallas kernels for 20%

profile of v1, /device:TPU:0, one launch (start us, length us, event | category | flops | bytes accessed | tf_op | source)
XLA Modules:
  0.0 109.6 jit_solution(804905975447061707)
XLA Ops:
  0.6 1.2 %dynamic_slice.18.length_ref = s32[1]{0:T(128)} dynamic-slice(s32[16]{0:T(128)} %param.6, s32[]{:T(128)S(6)} %select_n.50), dynamic_slice_sizes={1} | dynamic-slice | bytes 12 | tf_op jit(solution)/shard_map/dynamic_slice | solution.py:155
  1.9 0.9 dynamic-slice_bitcast_fusion
  2.8 59.4 %shard_map.77 = f32[80,1024]{1,0:T(8,128)S(1)} custom-call(s32[1]{0:T(128)} %dynamic_slice.18.length_ref, bf16[3,1536,1536]{2,1,0:T(8,128)(2,1)} %bitcast.24, bf16[3,1536,1536]{2,1,0:T(8,128)(2,1)} %bitcast.25, bf16[3,1536,1536]{2,1,0:T(8,128)(2,1)} %bitcast.26, bf16[72,1536]{1,0:T(8,128)(2,1)S(1)} %concatenate.10.w_ref), custom_call_target="tpu_custom_call" | custom-call | flops 19327352832 | bytes 14155776 | tf_op jit(solution)/shard_map/pallas_call | solution.py:134
  62.3 0.1 fusion
  62.4 3.0 %collective-permute-start.1 = (f32[66,512]{1,0:T(8,128)S(1)}, f32[66,512]{1,0:T(8,128)S(1)}, u32[]{:S(2)}, u32[]{:S(2)}) collective-permute-start(f32[66,512]{1,0:T(8,128)S(1)} %fusion), channel_id=1, source_target_pairs={{0,1},{1,0},{2,3},{3,2},{4,5},{5,4},{6,7},{7,6},{8,9},{9,8},{10,11... | collective-permute-start | bytes 405512 | tf_op jit(solution)/shard_map/ppermute | solution.py:179
  65.3 22.3 %shard_map.76 = bf16[512,1536]{1,0:T(8,128)(2,1)S(1)} custom-call(s32[1]{0:T(128)} %dynamic_slice.18.length_ref, bf16[3,1536,1536]{2,1,0:T(8,128)(2,1)} %bitcast.27, bf16[3,1536,1536]{2,1,0:T(8,128)(2,1)} %bitcast.28, bf16[3,1536,1536]{2,1,0:T(8,128)(2,1)} %bitcast.29), custom_call_target="tpu_custom_call" | custom-call | flops 9663676416 | bytes 14155776 | tf_op jit(solution)/shard_map/pallas_call | solution.py:115
  87.6 0.0 copy-start
  87.6 0.0 copy-start.1
  87.6 0.1 constant_dynamic-slice_fusion
  87.7 0.1 collective-permute-start
  87.8 0.8 copy-done
  88.6 0.2 convert_reduce_fusion
  88.8 0.0 collective-permute-done.1
  88.8 0.1 fusion.2
  88.9 0.1 fusion.8
  89.0 0.1 collective-permute-start.2
  89.8 0.5 collective-permute-done.2
  90.3 0.0 copy-done.1
  90.3 0.8 fusion.7
  91.1 15.8 %collective-permute-done = bf16[256,1536]{1,0:T(8,128)(2,1)} collective-permute-done((bf16[256,1536]{1,0:T(8,128)(2,1)S(1)}, bf16[256,1536]{1,0:T(8,128)(2,1)}, u32[]{:S(2)}, u32[]{:S(2)}) %collective-permute-start) | collective-permute-done | bytes 786464 | tf_op jit(solution)/shard_map/ppermute | solution.py:162
  106.9 1.4 %broadcast_select_fusion.1 = (bf16[256,1536]{1,0:T(8,128)(2,1)S(1)}, bf16[256,1536]{1,0:T(8,128)(2,1)S(1)}) fusion(bf16[256,1536]{1,0:T(8,128)(2,1)} %collective-permute-done, pred[]{:T(512)S(6)} %eq.8, bf16[512,1536]{1,0:T(8,128)(2,1)S(1)} %shard_map.76, s32[]{:T(128)S(6)} %select_n.51), kind=kLoop, calls=%fused_computation.3 | loop fusion | flops 786432 | bytes 3145733 | tf_op jit(solution)/shard_map/jit(_where)/select_n | solution.py:165
  108.3 1.3 %maximum_bitcast_fusion = bf16[1,256,3072]{2,1,0:T(8,128)(2,1)} fusion(bf16[256,1536]{1,0:T(8,128)(2,1)S(1)} %get-tuple-element.4, bf16[256,1536]{1,0:T(8,128)(2,1)S(1)} %get-tuple-element.3), kind=kLoop, calls=%fused_computation | loop fusion | flops 3145728 | bytes 3145728 | tf_op jit(solution)/shard_map/broadcast_in_dim | solution.py:197
  (4 shorter events, 0.1 us)
Async XLA Ops:
  62.4 26.4 %collective-permute-start.1 = (f32[66,512]{1,0:T(8,128)S(1)}, f32[66,512]{1,0:T(8,128)S(1)}, u32[]{:S(2)}, u32[]{:S(2)}) collective-permute-start(f32[66,512]{1,0:T(8,128)S(1)} %fusion), channel_id=1, source_target_pairs={{0,1},{1,0},{2,3},{3,2},{4,5},{5,4},{6,7},{7,6},{8,9},{9,8},{10,11... | collective-permute-start | bytes 405512 | tf_op jit(solution)/shard_map/ppermute | solution.py:179
  87.6 1.0 copy-start
  87.6 2.7 %copy-start.1 = (f32[1,512,64]{1,2,0:T(8,128)S(1)}, f32[1,512,64]{1,2,0:T(8,128)}, u32[]{:S(2)}) copy-start(f32[1,512,64]{1,2,0:T(8,128)} %param.8) | copy-start | bytes 393220
  87.7 19.2 %collective-permute-start = (bf16[256,1536]{1,0:T(8,128)(2,1)S(1)}, bf16[256,1536]{1,0:T(8,128)(2,1)}, u32[]{:S(2)}, u32[]{:S(2)}) collective-permute-start(bf16[256,1536]{1,0:T(8,128)(2,1)S(1)} %constant_dynamic-slice_fusion), channel_id=1, source_target_pairs={{0,1},{1,0},{2,3},{3,2},{4,5},{5,4},{6,7},{7,6},{8,9},{9,8},{10,11... | collective-permute-start | bytes 2359304 | tf_op jit(solution)/shard_map/ppermute | solution.py:162
  89.0 1.3 %collective-permute-start.2 = (bf16[64,512]{1,0:T(8,128)(2,1)S(1)}, bf16[64,512]{1,0:T(8,128)(2,1)S(1)}, u32[]{:S(2)}, u32[]{:S(2)}) collective-permute-start(bf16[64,512]{1,0:T(8,128)(2,1)S(1)} %fusion.8), channel_id=1, source_target_pairs={{0,2},{2,0},{4,6},{6,4},{8,10},{10,8},{12,14},{14,12},{16,18},{18,... | collective-permute-start | bytes 196616 | tf_op jit(solution)/shard_map/ppermute | solution.py:189

commit v2 on v1

v2 whole, which is shorter than its diff:
```python
import functools

import jax
import jax.numpy as jnp
from jax import lax
from jax.experimental import pallas as pl
from jax.experimental.pallas import tpu as pltpu
from jax.sharding import PartitionSpec as P

HD = 128
TXT = 512
NSTEPS = 28

guidance_scale = 3.5
plan_shift = 3.0
norm_eps = 1e-06

LOG2_SCALE = 1.4426950408889634 * HD ** (-0.5)
ROWS = 256
CONTRACT_LAST = (((1,), (1,)), ((), ()))


def sigma_at(step_value):
    remain = 1.0 - step_value / NSTEPS
    return plan_shift * remain / (1.0 + (plan_shift - 1.0) * remain)


def prepare_keys(text_length, k_ref, v_ref, kk, vv):
    seq = k_ref.shape[1]
    keys = k_ref[0]
    row = lax.broadcasted_iota(jnp.int32, (TXT, HD), 0)
    valid = row < text_length
    spare = jnp.broadcast_to(keys[TXT : TXT + 1].astype(jnp.float32), (TXT, HD))
    text_keys = jnp.where(valid, keys[:TXT].astype(jnp.float32), spare).astype(jnp.bfloat16)
    kk[:TXT, :HD] = text_keys
    kk[:TXT, HD:] = text_keys
    kk[TXT:, :HD] = keys[TXT:]
    kk[TXT:, HD:] = keys[TXT:]
    text_values = jnp.where(valid, v_ref[0, :TXT].astype(jnp.float32), 0.0)
    vv[:TXT, :HD] = text_values.astype(jnp.bfloat16)
    vv[:TXT, HD:] = jnp.where(valid, 1.0, 0.0).astype(jnp.bfloat16)
    vv[TXT:, :HD] = v_ref[0, TXT:]
    vv[TXT:, HD:] = jnp.ones((seq - TXT, HD), jnp.bfloat16)


def score_block(query, kk):
    scaled = query.astype(jnp.float32) * LOG2_SCALE
    high = scaled.astype(jnp.bfloat16)
    low = (scaled - high.astype(jnp.float32)).astype(jnp.bfloat16)
    both = jnp.concatenate([high, low], axis=1)
    return lax.dot_general(both, kk[...], CONTRACT_LAST, preferred_element_type=jnp.float32)


def weigh(scores, vv):
    row_max = jnp.max(scores, axis=1, keepdims=True)
    weights = jnp.exp2(scores - row_max).astype(jnp.bfloat16)
    summed = jnp.dot(weights, vv[...], preferred_element_type=jnp.float32)
    return (summed[:, :HD] / summed[:, HD:]).astype(jnp.bfloat16)


def attend_group(text_length, q_ref, k_ref, v_ref, kk, vv, first, count, finish):
    heads = q_ref.shape[2] // HD
    tasks = [(h, r) for h in range(heads) for r in range(0, count, ROWS)]

    def scores_of(task):
        head, row = task
        lanes = pl.ds(head * HD, HD)
        if row == 0:
            prepare_keys(
                text_length,
                k_ref.at[:, :, lanes],
                v_ref.at[:, :, lanes],
                kk.at[head],
                vv.at[head],
            )
        return score_block(q_ref[0, first + row : first + row + ROWS, lanes], kk.at[head])

    scores = scores_of(tasks[0])
    for index, (head, row) in enumerate(tasks):
        later = scores_of(tasks[index + 1]) if index + 1 < len(tasks) else None
        finish(head, row, weigh(scores, vv.at[head]))
        scores = later


def text_kernel(length_ref, q_ref, k_ref, v_ref, out_ref, kk, vv):
    text_length = length_ref[lax.axis_index("batch")]

    def finish(head, row, result):
        place = row + lax.broadcasted_iota(jnp.int32, (ROWS, HD), 0)
        kept = jnp.where(place < text_length, result.astype(jnp.float32), 0.0)
        out_ref[row : row + ROWS, head * HD : (head + 1) * HD] = kept.astype(jnp.bfloat16)

    attend_group(text_length, q_ref, k_ref, v_ref, kk, vv, 0, TXT, finish)


def image_kernel(length_ref, q_ref, k_ref, v_ref, w_ref, out_ref, col_ref, kk, vv, held):
    image = out_ref.shape[1]
    steps, _, group = held.shape
    width = steps * group
    step = pl.program_id(0)

    def finish(head, row, result):
        held[step, row : row + ROWS, head * HD : (head + 1) * HD] = result

    text_length = length_ref[lax.axis_index("batch")]
    attend_group(text_length, q_ref, k_ref, v_ref, kk, vv, TXT, image, finish)

    @pl.when(step == steps - 1)
    def _():
        total = jnp.sum(w_ref[...].astype(jnp.float32), axis=1, keepdims=True)
        col_ref[...] = jnp.broadcast_to(total, col_ref.shape)
        start = pl.multiple_of(lax.axis_index("tensor") * width, HD)
        own = w_ref[:, pl.ds(start, width)]
        own = jnp.concatenate([own, jnp.ones((8, width), jnp.bfloat16)], axis=0)
        for row in range(0, image, ROWS):
            span = slice(row, row + ROWS)
            product = jnp.zeros((72, ROWS), jnp.float32)
            square = jnp.zeros((ROWS, HD), jnp.float32)
            for part in range(steps):
                tokens = held[part, span, :]
                product += lax.dot_general(
                    own[:, part * group : (part + 1) * group],
                    tokens,
                    CONTRACT_LAST,
                    preferred_element_type=jnp.float32,
                )
                for lane in range(0, group, HD):
                    wide = tokens[:, lane : lane + HD].astype(jnp.float32)
                    square += wide * wide
            out_ref[:72, span] = product
            squares = jnp.sum(jnp.transpose(square), axis=0, keepdims=True)
            out_ref[72:, span] = jnp.broadcast_to(squares, (8, ROWS))


def grouping(width):
    heads = width // HD
    together = 3 if heads % 3 == 0 else 1
    return heads // together, together * HD


def head_specs(seq, group):
    def part(which):
        return pl.BlockSpec((1, seq, group), lambda h, length: (which, 0, h))

    return [part(0), part(1), part(2)]


def scratch(seq, group):
    shape = (group // HD, seq, 2 * HD)
    return [pltpu.VMEM(shape, jnp.bfloat16), pltpu.VMEM(shape, jnp.bfloat16)]


def cost(width, rows, seq):
    return pl.CostEstimate(
        flops=8 * rows * seq * width,
        bytes_accessed=6 * seq * width,
        transcendentals=width // HD * rows * seq,
    )


def attend_text(lengths, local):
    seq, width = local.shape[1:]
    steps, group = grouping(width)
    return pl.pallas_call(
        text_kernel,
        grid_spec=pltpu.PrefetchScalarGridSpec(
            num_scalar_prefetch=1,
            grid=(steps,),
            in_specs=head_specs(seq, group),
            out_specs=pl.BlockSpec((TXT, group), lambda h, length: (0, h)),
            scratch_shapes=scratch(seq, group),
        ),
        out_shape=jax.ShapeDtypeStruct((TXT, width), jnp.bfloat16),
        compiler_params=pltpu.CompilerParams(vmem_limit_bytes=48 * 2**20),
        cost_estimate=cost(width, TXT, seq),
    )(lengths, local, local, local)


def attend_image(lengths, local, weight):
    seq, width = local.shape[1:]
    steps, group = grouping(width)
    image = seq - TXT
    lanes, depth = weight.shape
    return pl.pallas_call(
        image_kernel,
        grid_spec=pltpu.PrefetchScalarGridSpec(
            num_scalar_prefetch=1,
            grid=(steps,),
            in_specs=head_specs(seq, group)
            + [pl.BlockSpec((lanes, depth), lambda h, length: (0, 0))],
            out_specs=[
                pl.BlockSpec((80, image), lambda h, length: (0, 0)),
                pl.BlockSpec((lanes, HD), lambda h, length: (0, 0)),
            ],
            scratch_shapes=scratch(seq, group) + [pltpu.VMEM((steps, image, group), jnp.bfloat16)],
        ),
        out_shape=[
            jax.ShapeDtypeStruct((80, image), jnp.float32),
            jax.ShapeDtypeStruct((lanes, HD), jnp.float32),
        ],
        compiler_params=pltpu.CompilerParams(vmem_limit_bytes=48 * 2**20),
        cost_estimate=cost(width, image, seq),
    )(lengths, local, local, local, weight)


def per_device(qkv, text_len, step_idx, latent, w_out):
    local = jnp.transpose(qkv[0], (1, 0, 2))
    shares = lax.axis_size("tensor")
    position = lax.axis_index("batch")
    share = lax.axis_index("tensor")

    text_out = attend_text(text_len, local)
    text_rows = TXT // shares
    if shares == 2:
        text_kept = lax.dynamic_slice_in_dim(text_out, share * text_rows, text_rows)
        sent = lax.dynamic_slice_in_dim(text_out, (1 - share) * text_rows, text_rows)
        text_came = lax.ppermute(sent, "tensor", [(0, 1), (1, 0)])
    else:
        text_tokens = lax.all_to_all(text_out, "tensor", split_axis=0, concat_axis=1, tiled=True)

    weight_t = jnp.transpose(w_out)
    weight_t, text_out = lax.optimization_barrier((weight_t, text_out))
    sums, colsum = attend_image(text_len, local, weight_t)
    sums = jnp.concatenate([sums[:65], sums[72:73]], axis=0)
    if shares == 2:
        sums, came = lax.optimization_barrier((sums, text_came))
        first = share == 0
        text_tokens = jnp.concatenate(
            [jnp.where(first, text_kept, came), jnp.where(first, came, text_kept)], axis=1
        )
    image_rows = sums.shape[1] // shares
    if shares == 2:
        kept = lax.dynamic_slice_in_dim(sums, share * image_rows, image_rows, axis=1)
        sent = lax.dynamic_slice_in_dim(sums, (1 - share) * image_rows, image_rows, axis=1)
        total = kept + lax.ppermute(sent, "tensor", [(0, 1), (1, 0)])
    else:
        total = lax.psum_scatter(sums, "tensor", scatter_dimension=1, tiled=True)

    depth = w_out.shape[0]
    colsum = colsum[:, :1]
    row_mean = total[64:65] / depth
    row_meansq = total[65:66] / depth
    raw = (total[:64] - row_mean * colsum) * lax.rsqrt(row_meansq - row_mean * row_mean + norm_eps)
    pairs = [(source, source ^ 1) for source in range(lax.axis_size("batch"))]
    partner = lax.ppermute(raw.astype(jnp.bfloat16), "batch", pairs).astype(jnp.float32)
    is_cond = position % 2 == 0
    cond_velocity = jnp.where(is_cond, raw, partner)
    uncond_velocity = jnp.where(is_cond, partner, raw)
    guided = uncond_velocity + guidance_scale * (cond_velocity - uncond_velocity)
    step_value = step_idx[0].astype(jnp.float32)
    step_delta = sigma_at(step_value + 1.0) - sigma_at(step_value)
    updated = jnp.transpose(latent[0]) + step_delta * guided
    return (text_tokens[None], jnp.transpose(guided)[None], jnp.transpose(updated)[None])


def solution(mesh):
    placed = (P("batch", None, None, "tensor"), P(), P("batch"), P("batch", "tensor", None), P())
    return jax.shard_map(
        per_device,
        mesh=mesh,
        in_specs=placed,
        out_specs=(
            P("batch", "tensor", None),
            P("batch", "tensor", None),
            P("batch", "tensor", None),
        ),
        check_vma=False,
    )
```

time: 110 us -> 57.1 us (0.52)
  Pallas kernels: 81.6 us -> 43.7 us
  waiting for transfers between devices: 16.3 us -> 4.16 us
  local copies, waits for them, and re-layouts: 3.12 us -> 0.87 us
  other arithmetic: 3.98 us -> 2.62 us
    pallas_call x1, Pallas kernels: 59.4 us -> 27.4 us  [attend_image(): pl.pallas_call(image_kernel, grid_spec=pltpu.PrefetchScalarGridSpec(num_s...]
    ppermute x1, waiting for transfers between devices: 15.8 us -> 0.01 us  [per_device(): text_came = lax.ppermute(sent, 'tensor', [(0, 1), (1, 0)])]
    pallas_call x1, Pallas kernels: 22.3 us -> 16.3 us  [attend_text(): pl.pallas_call(text_kernel, grid_spec=pltpu.PrefetchScalarGridSpec(num_sc...]
    ppermute x1, waiting for transfers between devices: 0.01 us -> 4.15 us  [per_device(): total = kept + lax.ppermute(sent, 'tensor', [(0, 1), (1, 0)])]
    ppermute x1, starting transfers between devices: 0.08 us -> 3.03 us  [per_device(): text_came = lax.ppermute(sent, 'tensor', [(0, 1), (1, 0)])]
    dynamic_slice x2 -> x1, local copies, waits for them, and re-layouts: 2.18 us -> 0.02 us  [per_device(): lax.dynamic_slice_in_dim(sums, (1 - share) * image_rows, image_rows, axis=1)]
    ppermute x1, starting transfers between devices: 2.98 us -> 0.91 us  [per_device(): total = kept + lax.ppermute(sent, 'tensor', [(0, 1), (1, 0)])]
  transfers between devices with their start and end apart: 3 -> 3, of which waited for: 2 -> 1; matrix products, arithmetic and copies ran while one was open for 1% -> 3% of each run, Pallas kernels for 20% -> 48%
where the time goes in v2:
time: 57.1 us; the launch traced here: 56.9 us
  Pallas kernels  43.7 us (77%)
  waiting for transfers between devices  4.16 us (7%)
  starting transfers between devices  4.01 us (7%)
  other arithmetic  2.62 us (5%)
  between operations  1.52 us (3%)
  local copies, waits for them, and re-layouts  0.87 us (2%)
    pallas_call x1, Pallas kernels, attend_image(): pl.pallas_call(image_kernel, grid_spec=pltpu.PrefetchScalarGridSpec(num_s...  27.4 us
    pallas_call x1, Pallas kernels, attend_text(): pl.pallas_call(text_kernel, grid_spec=pltpu.PrefetchScalarGridSpec(num_sc...  16.3 us
    ppermute x1, waiting for transfers between devices, per_device(): total = kept + lax.ppermute(sent, 'tensor', [(0, 1), (1, 0)])  4.15 us
    ppermute x1, starting transfers between devices, per_device(): text_came = lax.ppermute(sent, 'tensor', [(0, 1), (1, 0)])  3.03 us
    broadcast_in_dim x1, other arithmetic, per_device(): text_tokens[None]  1.35 us
  transfers between devices with their start and end apart: 3, of which 1 were waited for; matrix products, arithmetic and copies ran while one was open for 3% of the time, Pallas kernels for 48%

profile of v2, /device:TPU:0, one launch (start us, length us, event | category | flops | bytes accessed | tf_op | source)
XLA Modules:
  0.0 56.9 jit_solution(7495439694012953690)
XLA Ops:
  0.6 0.0 copy-start
  0.6 0.6 %copy-done = s32[16]{0:T(128)S(1)} copy-done((s32[16]{0:T(128)S(1)}, s32[16]{0:T(128)}, u32[]{:S(2)}) %copy-start) | copy-done | bytes 88
  1.3 16.3 %shard_map.76 = bf16[512,1536]{1,0:T(8,128)(2,1)S(1)} custom-call(s32[16]{0:T(128)S(1)} %copy-done, bf16[3,1536,1536]{2,1,0:T(8,128)(2,1)} %bitcast.24, bf16[3,1536,1536]{2,1,0:T(8,128)(2,1)} %bitcast.25, bf16[3,1536,1536]{2,1,0:T(8,128)(2,1)} %bitcast.26), custom_call_target="tpu_custom_call" | custom-call | flops 9663676416 | bytes 14155776 | tf_op jit(solution)/shard_map/pallas_call | solution.py:164
  17.6 0.0 copy-start.1
  17.7 0.1 constant_dynamic-slice_fusion.1
  17.7 3.0 %collective-permute-start = (bf16[256,1536]{1,0:T(8,128)(2,1)S(1)}, bf16[256,1536]{1,0:T(8,128)(2,1)S(1)}, u32[]{:S(2)}, u32[]{:S(2)}) collective-permute-start(bf16[256,1536]{1,0:T(8,128)(2,1)S(1)} %constant_dynamic-slice_fusion.1), channel_id=1, source_target_pairs={{0,1},{1,0},{2,3},{3,2},{4,5},{5,4},{6,7},{7,6},{8,9},{9,8},{10,11... | collective-permute-start | bytes 2359304 | tf_op jit(solution)/shard_map/ppermute | solution.py:217
  20.8 0.0 copy-done.1
  20.8 27.4 %shard_map.77 = (f32[80,1024]{1,0:T(8,128)S(1)}, f32[64,128]{1,0:T(8,128)S(1)}) custom-call(s32[16]{0:T(128)S(1)} %copy-done, bf16[3,1536,1536]{2,1,0:T(8,128)(2,1)} %bitcast.27, bf16[3,1536,1536]{2,1,0:T(8,128)(2,1)} %bitcast.28, bf16[3,1536,1536]{2,1,0:T(8,128)(2,1)} %bitcast.29, bf16[64,3072]{1,0:T(8,128)(2,1)S(1)} %bitcast.23), custom_call_target="tpu_custom_call" | custom-call | flops 19327352832 | bytes 14155776 | tf_op jit(solution)/shard_map/pallas_call | solution.py:184
  48.9 0.1 slice_reduce_fusion
  49.1 0.0 collective-permute-done
  49.1 0.9 %collective-permute-start.1 = (f32[66,512]{1,0:T(8,128)S(1)}, f32[66,512]{1,0:T(8,128)S(1)}, u32[]{:S(2)}, u32[]{:S(2)}) collective-permute-start(f32[66,512]{1,0:T(8,128)S(1)} %constant_dynamic-slice_fusion), channel_id=1, source_target_pairs={{0,1},{1,0},{2,3},{3,2},{4,5},{5,4},{6,7},{7,6},{8,9},{9,8},{10,11... | collective-permute-start | bytes 405512 | tf_op jit(solution)/shard_map/ppermute | solution.py:235
  50.0 0.3 broadcast_select_fusion.1
  50.3 4.2 %collective-permute-done.1 = f32[66,512]{1,0:T(8,128)S(1)} collective-permute-done((f32[66,512]{1,0:T(8,128)S(1)}, f32[66,512]{1,0:T(8,128)S(1)}, u32[]{:S(2)}, u32[]{:S(2)}) %collective-permute-start.1) | collective-permute-done | bytes 135200 | tf_op jit(solution)/shard_map/ppermute | solution.py:235
  54.5 0.1 fusion.5
  54.6 0.1 collective-permute-start.2
  54.7 0.0 copy-start.2
  54.7 1.3 %maximum_bitcast_fusion = bf16[1,256,3072]{2,1,0:T(8,128)(2,1)} fusion(bf16[256,1536]{1,0:T(8,128)(2,1)S(1)} %get-tuple-element.14, bf16[256,1536]{1,0:T(8,128)(2,1)S(1)} %get-tuple-element.13), kind=kLoop, calls=%fused_computation | loop fusion | flops 3145728 | bytes 3145728 | tf_op jit(solution)/shard_map/broadcast_in_dim | solution.py:253
  56.1 0.0 collective-permute-done.2
  56.1 0.0 copy-done.2
  56.1 0.8 %fusion.4 = (f32[1,512,64]{1,2,0:T(8,128)}, f32[1,512,64]{1,2,0:T(8,128)}) fusion(f32[1,512,64]{1,2,0:T(8,128)S(1)} %copy-done.2, f32[]{:T(128)} %bitcast.11, f32[512]{0:T(512)S(1)} %bitcast.33, f32[64]{0:T(128)S(1)} %slice_reduce_fusion, f32[512]{0:T(512)S(1)} %bitcast.31, f32[66,512]{1,0:T(8,128)S(1)} %dynamic-slice_add_fusion, ...), kind=kLoop, calls=%fused_computation.13 | loop fusion | flops 360448 | bytes 594181 | tf_op jit(solution)/shard_map/broadcast_in_dim | solution.py:253
  (6 shorter events, 0.1 us)
Async XLA Ops:
  0.6 0.7 %copy-start = (s32[16]{0:T(128)S(1)}, s32[16]{0:T(128)}, u32[]{:S(2)}) copy-start(s32[16]{0:T(128)} %length_ref.3) | copy-start | bytes 196
  17.6 3.1 %copy-start.1 = (bf16[3072,64]{0,1:T(8,128)(2,1)S(1)}, bf16[3072,64]{0,1:T(8,128)(2,1)}, u32[]{:S(2)}) copy-start(bf16[3072,64]{0,1:T(8,128)(2,1)} %param.9) | copy-start | bytes 1179652
  17.7 31.4 %collective-permute-start = (bf16[256,1536]{1,0:T(8,128)(2,1)S(1)}, bf16[256,1536]{1,0:T(8,128)(2,1)S(1)}, u32[]{:S(2)}, u32[]{:S(2)}) collective-permute-start(bf16[256,1536]{1,0:T(8,128)(2,1)S(1)} %constant_dynamic-slice_fusion.1), channel_id=1, source_target_pairs={{0,1},{1,0},{2,3},{3,2},{4,5},{5,4},{6,7},{7,6},{8,9},{9,8},{10,11... | collective-permute-start | bytes 2359304 | tf_op jit(solution)/shard_map/ppermute | solution.py:217
  49.1 5.4 %collective-permute-start.1 = (f32[66,512]{1,0:T(8,128)S(1)}, f32[66,512]{1,0:T(8,128)S(1)}, u32[]{:S(2)}, u32[]{:S(2)}) collective-permute-start(f32[66,512]{1,0:T(8,128)S(1)} %constant_dynamic-slice_fusion), channel_id=1, source_target_pairs={{0,1},{1,0},{2,3},{3,2},{4,5},{5,4},{6,7},{7,6},{8,9},{9,8},{10,11... | collective-permute-start | bytes 405512 | tf_op jit(solution)/shard_map/ppermute | solution.py:235
  54.6 1.4 %collective-permute-start.2 = (bf16[64,512]{1,0:T(8,128)(2,1)S(1)}, bf16[64,512]{1,0:T(8,128)(2,1)S(1)}, u32[]{:S(2)}, u32[]{:S(2)}) collective-permute-start(bf16[64,512]{1,0:T(8,128)(2,1)S(1)} %fusion.5), channel_id=1, source_target_pairs={{0,2},{2,0},{4,6},{6,4},{8,10},{10,8},{12,14},{14,12},{16,18},{18,... | collective-permute-start | bytes 196616 | tf_op jit(solution)/shard_map/ppermute | solution.py:245
  54.7 1.4 %copy-start.2 = (f32[1,512,64]{1,2,0:T(8,128)S(1)}, f32[1,512,64]{1,2,0:T(8,128)}, u32[]{:S(2)}) copy-start(f32[1,512,64]{1,2,0:T(8,128)} %param.8) | copy-start | bytes 393220
